TPU v7x, 256 devices: a whole 4x4x8 slice. The times are simulated.
256 devices in a mesh: dp: 16 (over z_lo, x), uly: 4 (over z_hi, core), blk: 4 (over y).
Axes of the slice: x: 4, y: 4, z: 8 (z_hi: 2, z_lo: 4; z = z_hi * 4 + z_lo), core: 2. Of those that a mesh axis runs over, the one named last changes fastest.
Arguments:
- query_rows: bfloat16 [16, 2048, 2560], P('dp', ('uly', 'blk')), may hold values from -6.5 to 6.5, as said below
- key_rows: bfloat16 [16, 2048, 2560], P('dp', ('uly', 'blk')), may hold values from -4 to 4, as said below
- value_rows: bfloat16 [16, 2048, 2560], P('dp', ('uly', 'blk')), may hold values from -6 to 6
- query_tangent: bfloat16 [16, 2048, 2560], P('dp', ('uly', 'blk')), may hold values from -6 to 6
- key_tangent: bfloat16 [16, 2048, 2560], P('dp', ('uly', 'blk')), may hold values from -6 to 6
- value_tangent: bfloat16 [16, 2048, 2560], P('dp', ('uly', 'blk')), may hold values from -6 to 6
- out_weight: bfloat16 [2560, 5120], P('uly', ('blk', 'dp')), may hold values from -0.125 to 0.125
Outputs:
- mixed: bfloat16 [16, 2048, 5120], P('dp', ('uly', 'blk'))
- mixed_tangent: bfloat16 [16, 2048, 5120], P('dp', ('uly', 'blk'))
Inputs may be any that keep to these rules, and one draw needn't show every extreme that they name: `query_rows`: queries of unit-scale entries. `key_rows`: keys of unit-scale entries.
All inputs are finite; a program needn't handle non-finite values.
Results may differ from a plain program's by a relative error of at most 0.019.
Values may be sent and summed in bfloat16 or wider, within the bound.
A program may use at most 128 MiB of HBM per device.

v0:
```python
import jax
import jax.numpy as jnp
from jax import lax
from jax.sharding import PartitionSpec as P

HEAD_DIM = 128


LOW_START = -1e30


def block_update(carry, query, query_tan, block):
    top, total, spread, plain, carried = carry
    key, value, key_tan, value_tan = block
    factor = HEAD_DIM ** (-0.5)
    scores = jnp.einsum("qhd,khd->hqk", query, key, preferred_element_type=jnp.float32) * factor
    score_tan = (
        jnp.einsum("qhd,khd->hqk", query_tan, key, preferred_element_type=jnp.float32)
        + jnp.einsum("qhd,khd->hqk", query, key_tan, preferred_element_type=jnp.float32)
    ) * factor
    newtop = jnp.maximum(top, jnp.max(scores, axis=2))
    shrink = jnp.exp(top - newtop)
    weights = jnp.exp(scores - newtop[:, :, None])
    moved = weights * score_tan
    total = total * shrink + jnp.sum(weights, axis=2)
    spread = spread * shrink + jnp.sum(moved, axis=2)
    weights_low = weights.astype(jnp.bfloat16)
    moved_low = moved.astype(jnp.bfloat16)
    factor_rows = shrink.T[:, :, None]
    plain = plain * factor_rows + jnp.einsum(
        "hqk,khd->qhd", weights_low, value, preferred_element_type=jnp.float32
    )
    carried = (
        carried * factor_rows
        + jnp.einsum("hqk,khd->qhd", moved_low, value, preferred_element_type=jnp.float32)
        + jnp.einsum("hqk,khd->qhd", weights_low, value_tan, preferred_element_type=jnp.float32)
    )
    return (newtop, total, spread, plain, carried)


def per_device(
    query_rows, key_rows, value_rows, query_tangent, key_tangent, value_tangent, out_weight
):
    moved_in = (
        lax.all_to_all(query_rows, "uly", split_axis=2, concat_axis=1, tiled=True),
        lax.all_to_all(key_rows, "uly", split_axis=2, concat_axis=1, tiled=True),
        lax.all_to_all(value_rows, "uly", split_axis=2, concat_axis=1, tiled=True),
        lax.all_to_all(query_tangent, "uly", split_axis=2, concat_axis=1, tiled=True),
        lax.all_to_all(key_tangent, "uly", split_axis=2, concat_axis=1, tiled=True),
        lax.all_to_all(value_tangent, "uly", split_axis=2, concat_axis=1, tiled=True),
    )
    query, key, value, query_tan, key_tan, value_tan = [
        item.reshape(-1, item.shape[-1]) for item in moved_in
    ]
    rows_here = query.shape[0]
    width_here = query.shape[1]
    heads_here = width_here // HEAD_DIM
    query_h = query.reshape(rows_here, heads_here, HEAD_DIM)
    query_tan_h = query_tan.reshape(rows_here, heads_here, HEAD_DIM)
    start_carry = (
        jnp.full((heads_here, rows_here), LOW_START, jnp.float32),
        jnp.zeros((heads_here, rows_here), jnp.float32),
        jnp.zeros((heads_here, rows_here), jnp.float32),
        jnp.zeros((rows_here, heads_here, HEAD_DIM), jnp.float32),
        jnp.zeros((rows_here, heads_here, HEAD_DIM), jnp.float32),
    )
    piece = (
        lax.all_gather(key, "blk", axis=0, tiled=True),
        lax.all_gather(value, "blk", axis=0, tiled=True),
        lax.all_gather(key_tan, "blk", axis=0, tiled=True),
        lax.all_gather(value_tan, "blk", axis=0, tiled=True),
    )
    arrays = tuple((item.reshape(-1, heads_here, HEAD_DIM) for item in piece))
    count = arrays[0].shape[0]
    blocks = tuple((item.reshape(count // 512, 512, heads_here, HEAD_DIM) for item in arrays))

    def scan_step(inner, block):
        return (block_update(inner, query_h, query_tan_h, block), None)

    result, unused = lax.scan(scan_step, start_carry, blocks)
    top, total, spread, plain, carried = result
    total_rows = total.T[:, :, None]
    spread_rows = spread.T[:, :, None]
    attended = (plain / total_rows).reshape(rows_here, width_here).astype(jnp.bfloat16)
    attended_tan = (carried - spread_rows / total_rows * plain) / total_rows
    attended_tan = attended_tan.reshape(rows_here, width_here).astype(jnp.bfloat16)
    column_block = lax.all_gather(out_weight, "dp", axis=1, tiled=True)
    stacked = jnp.concatenate([attended, attended_tan], axis=0)
    terms = jnp.dot(
        stacked,
        lax.all_gather(column_block, "blk", axis=1, tiled=True),
        preferred_element_type=jnp.float32,
    )
    width_out = terms.shape[1]
    sums = lax.psum_scatter(
        terms.reshape(2, rows_here, width_out).astype(jnp.bfloat16),
        "uly",
        scatter_dimension=1,
        tiled=True,
    ).astype(jnp.float32)
    mixed = sums[0]
    mixed_tangent = sums[1]
    return (mixed[None].astype(jnp.bfloat16), mixed_tangent[None].astype(jnp.bfloat16))


def solution(mesh):
    return jax.shard_map(
        per_device,
        mesh=mesh,
        in_specs=(
            P("dp", ("uly", "blk"), None),
            P("dp", ("uly", "blk"), None),
            P("dp", ("uly", "blk"), None),
            P("dp", ("uly", "blk"), None),
            P("dp", ("uly", "blk"), None),
            P("dp", ("uly", "blk"), None),
            P("uly", ("blk", "dp")),
        ),
        out_specs=(P("dp", ("uly", "blk"), None), P("dp", ("uly", "blk"), None)),
        check_vma=False,
    )
```

profile of v0, /device:TPU:1, one launch (start us, length us, event | category | flops | bytes accessed | tf_op | source)
XLA Modules:
  0.0 549.8 jit_solution(4954754931381398055)
XLA Ops:
  7.9 2.5 copy.78
  11.1 14.3 %reduce = bf16[2560,128]{1,0:T(8,128)(2,1)S(1)} reduce(bf16[2560,1,128]{2,1,0:T(2,128)(2,1)S(1)} %bitcast.136, bf16[]{:T(256)} %broadcast.72), dimensions={1}, to_apply=%bitcast.78.reduce_sub_computation | reduce | bytes 1310722
  25.5 27.3 %all_to_all.90 = bf16[4,2,40960]{2,1,0:T(2,128)(2,1)S(1)} all-to-all(bf16[4,2,40960]{2,1,0:T(2,128)(2,1)S(1)} %reshape.41), channel_id=1, replica_groups=mesh['dp'=16,'uly'=4,'blk'=4] {'uly'}, dimensions={0} | all-to-all | bytes 1310720 | tf_op jit(solution)/shard_map/all_to_all | solution.py:46
  53.6 1.1 copy.79
  54.7 1.0 copy.85
  55.7 14.3 %reduce.3 = bf16[2560,128]{1,0:T(8,128)(2,1)S(1)} reduce(bf16[2560,1,128]{2,1,0:T(2,128)(2,1)S(1)} %bitcast.138, bf16[]{:T(256)} %broadcast.72), dimensions={1}, to_apply=%bitcast.84.reduce_sub_computation | reduce | bytes 1310722
  70.2 18.7 %all_to_all.91 = bf16[4,2,40960]{2,1,0:T(2,128)(2,1)S(1)} all-to-all(bf16[4,2,40960]{2,1,0:T(2,128)(2,1)S(1)} %reshape.47), channel_id=1, replica_groups=mesh['dp'=16,'uly'=4,'blk'=4] {'uly'}, dimensions={0} | all-to-all | bytes 1310720 | tf_op jit(solution)/shard_map/all_to_all | solution.py:49
  89.6 1.1 copy.86
  91.0 1.0 copy.88
  91.9 14.3 %reduce.4 = bf16[2560,128]{1,0:T(8,128)(2,1)S(1)} reduce(bf16[2560,1,128]{2,1,0:T(2,128)(2,1)S(1)} %bitcast.139, bf16[]{:T(256)} %broadcast.72), dimensions={1}, to_apply=%bitcast.86.reduce_sub_computation | reduce | bytes 1310722
  106.4 16.1 %all_to_all.92 = bf16[4,2,40960]{2,1,0:T(2,128)(2,1)S(1)} all-to-all(bf16[4,2,40960]{2,1,0:T(2,128)(2,1)S(1)} %reshape.49), channel_id=1, replica_groups=mesh['dp'=16,'uly'=4,'blk'=4] {'uly'}, dimensions={0} | all-to-all | bytes 1310720 | tf_op jit(solution)/shard_map/all_to_all | solution.py:47
  123.3 1.1 copy.89
  125.4 14.3 %reduce.5 = bf16[2560,128]{1,0:T(8,128)(2,1)S(1)} reduce(bf16[2560,1,128]{2,1,0:T(2,128)(2,1)S(1)} %bitcast.140, bf16[]{:T(256)} %broadcast.72), dimensions={1}, to_apply=%bitcast.88.reduce_sub_computation | reduce | bytes 1310722
  139.9 16.8 %all_to_all.93 = bf16[4,2,40960]{2,1,0:T(2,128)(2,1)S(1)} all-to-all(bf16[4,2,40960]{2,1,0:T(2,128)(2,1)S(1)} %reshape.51), channel_id=1, replica_groups=mesh['dp'=16,'uly'=4,'blk'=4] {'uly'}, dimensions={0} | all-to-all | bytes 1310720 | tf_op jit(solution)/shard_map/all_to_all | solution.py:50
  157.4 1.1 copy.92
  159.5 14.4 %reduce.1 = bf16[2560,128]{1,0:T(8,128)(2,1)S(1)} reduce(bf16[2560,1,128]{2,1,0:T(2,128)(2,1)S(1)} %bitcast.141, bf16[]{:T(256)} %broadcast.72), dimensions={1}, to_apply=%bitcast.80.reduce_sub_computation | reduce | bytes 1310722
  173.9 1.0 reshape.43
  174.9 4.5 all-to-all-start.1
  180.3 14.3 %reduce.2 = bf16[2560,128]{1,0:T(8,128)(2,1)S(1)} reduce(bf16[2560,1,128]{2,1,0:T(2,128)(2,1)S(1)} %bitcast.137, bf16[]{:T(256)} %broadcast.72), dimensions={1}, to_apply=%bitcast.82.reduce_sub_computation | reduce | bytes 1310722
  194.6 1.0 reshape.45
  195.7 7.2 %all-to-all-start.2 = ((bf16[4,2,40960]{2,1,0:T(2,128)(2,1)}), bf16[4,2,40960]{2,1,0:T(2,128)(2,1)}, u32[]{:S(2)}, u32[]{:S(2)}) async-start(bf16[4,2,40960]{2,1,0:T(2,128)(2,1)} %reshape.45), calls=%async_computation.2 | async-start | bytes 1310720 | tf_op jit(solution)/shard_map/all_to_all | solution.py:48
  202.9 1.9 reshape.44
  204.8 1.4 copy.112
  206.7 1.1 reshape_reshape.19
  207.8 1.4 copy.95
  209.2 7.0 %all-to-all-done.2 = bf16[4,2,40960]{2,1,0:T(2,128)(2,1)} async-done(((bf16[4,2,40960]{2,1,0:T(2,128)(2,1)}), bf16[4,2,40960]{2,1,0:T(2,128)(2,1)}, u32[]{:S(2)}, u32[]{:S(2)}) %all-to-all-start.2) | async-done | bytes 655392 | tf_op jit(solution)/shard_map/all_to_all | solution.py:48
  216.3 3.6 reshape.46
  219.9 1.4 copy.113
  221.3 1.3 copy.84
  222.6 2.3 reshape_reshape.20
  224.9 2.2 copy.96
  227.6 7.0 %reshape.37 = bf16[4,512,5,128]{3,2,1,0:T(8,128)(2,1)} reshape(bf16[2048,640]{1,0:T(8,128)(2,1)} %all-gather.7.cloned.1.call-done) | data formatting | bytes 5242880 | tf_op jit(solution)/shard_map/reshape;reshape | solution.py:75
  234.6 4.6 copy.94
  239.2 7.0 %reshape.38 = bf16[4,512,5,128]{3,2,1,0:T(8,128)(2,1)} reshape(bf16[2048,640]{1,0:T(8,128)(2,1)} %all-gather.9.cloned.1.call-done) | data formatting | bytes 5242880 | tf_op jit(solution)/shard_map/reshape;reshape | solution.py:75
  246.2 4.4 copy.97
  250.6 7.0 %reshape.39 = bf16[4,512,5,128]{3,2,1,0:T(8,128)(2,1)} reshape(bf16[2048,640]{1,0:T(8,128)(2,1)} %all-gather.11.cloned.1.call-done) | data formatting | bytes 5242880 | tf_op jit(solution)/shard_map/reshape;reshape | solution.py:75
  257.6 7.0 %copy.98 = bf16[4,512,5,128]{1,3,2,0:T(8,128)(2,1)} copy(bf16[4,512,5,128]{3,2,1,0:T(8,128)(2,1)} %reshape.39) | data formatting | bytes 5242880
  264.6 7.0 %reshape.40 = bf16[4,512,5,128]{3,2,1,0:T(8,128)(2,1)} reshape(bf16[2048,640]{1,0:T(8,128)(2,1)} %all-gather.13.cloned.1.call-done) | data formatting | bytes 5242880 | tf_op jit(solution)/shard_map/reshape;reshape | solution.py:75
  271.6 7.2 %copy.99 = bf16[4,512,5,128]{1,3,2,0:T(8,128)(2,1)} copy(bf16[4,512,5,128]{3,2,1,0:T(8,128)(2,1)} %reshape.40) | data formatting | bytes 5242880
  278.8 61.0 %while.19 = (s32[]{:T(128)}, f32[5,512]{1,0:T(8,128)S(1)}, f32[5,512]{1,0:T(8,128)S(1)}, f32[5,512]{1,0:T(8,128)S(1)}, f32[512,5,128]{0,2,1:T(8,128)S(1)}, /*ind...) while((s32[]{:T(128)}, f32[5,512]{1,0:T(8,128)S(1)}, ...), condition=%wide.region_4.5_spmd.clone, body=%wide.region_0.4_spmd.clone.sunk | while | flops 2039173120 | bytes 87419088 | solution.py:80
  278.8 4.3 bitcast_reduce_fusion.2
  283.1 2.3 fusion.80
  286.0 3.0 fusion.81
  289.5 2.2 fusion.86
  291.8 1.4 fusion.84
  294.1 4.2 bitcast_reduce_fusion.2
  298.3 2.3 fusion.80
  301.3 3.0 fusion.81
  304.8 2.2 fusion.86
  307.1 1.4 fusion.84
  309.4 4.2 bitcast_reduce_fusion.2
  313.6 2.3 fusion.80
  316.6 3.0 fusion.81
  320.1 2.2 fusion.86
  322.4 1.4 fusion.84
  324.7 4.2 bitcast_reduce_fusion.2
  328.9 2.3 fusion.80
  331.8 3.0 fusion.81
  335.3 2.2 fusion.86
  337.6 1.4 fusion.84
  339.9 1.2 divide_convert_fusion.1
  341.1 14.0 %convolution_convert_fusion = bf16[1024,5120]{1,0:T(8,128)(2,1)} fusion(bf16[640,5120]{0,1:T(8,128)(2,1)} %all-gather.17.cloned.1.call-done, bf16[512,640]{0,1:T(8,128)(2,1)} %bitcast.160, bf16[512,640]{0,1:T(8,128)(2,1)S(1)} %bitcast.159), kind=kOutput, calls=%fused_computation.45 | convolution fusion | flops 6718750720 | bytes 18350080 | tf_op jit(solution)/shard_map/dot_general | solution.py:89
  355.1 184.3 %reduce-scatter.2.cloned.1.call-done = bf16[2,128,5120]{2,1,0:T(8,128)(2,1)} async-done(((bf16[2,512,5120]{2,1,0:T(8,128)(2,1)}), bf16[2,128,5120]{2,1,0:T(8,128)(2,1)}) %reduce-scatter.2.cloned.1.call-update) | async-done | bytes 2621456 | tf_op jit(solution)/shard_map/reduce_scatter | solution.py:95
  539.4 3.4 fusion.45
  (90 shorter events, 17.3 us)
Async XLA Ops:
  7.2 219.9 %all-gather.15.cloned.1.call-start = ((), (), s32[]{:S(2)}) async-start(), calls=%async_computation.11 | async-start | bytes 1740800 | tf_op jit(solution)/shard_map/all_gather | solution.py:87
  7.9 219.7 %all-gather.7.cloned.1.call-start = ((), (), s32[]{:S(2)}) async-start(), calls=%async_computation.7 | async-start | bytes 3276800 | tf_op jit(solution)/shard_map/all_gather | solution.py:68
  52.8 1.9 copy-start.2
  54.7 184.5 %all-gather.9.cloned.1.call-start = ((), (), s32[]{:S(2)}) async-start(), calls=%async_computation.8 | async-start | bytes 3276800 | tf_op jit(solution)/shard_map/all_gather | solution.py:70
  88.9 2.1 copy-start.3
  90.7 159.8 %all-gather.11.cloned.1.call-start = ((), (), s32[]{:S(2)}) async-start(), calls=%async_computation.9 | async-start | bytes 3276800 | tf_op jit(solution)/shard_map/all_gather | solution.py:69
  122.5 1.9 copy-start.4
  124.4 140.2 %all-gather.13.cloned.1.call-start = ((), (), s32[]{:S(2)}) async-start(), calls=%async_computation.10 | async-start | bytes 3276800 | tf_op jit(solution)/shard_map/all_gather | solution.py:71
  156.7 1.9 copy-start.5
  159.5 19.9 %copy-start.6 = (bf16[1,128,2560]{2,1,0:T(8,128)(2,1)S(1)}, bf16[1,128,2560]{2,1,0:T(8,128)(2,1)}, u32[]{:S(2)}) copy-start(bf16[1,128,2560]{2,1,0:T(8,128)(2,1)} %param.12) | copy-start | bytes 1966084
  174.9 20.8 %all-to-all-start.1 = ((bf16[4,2,40960]{2,1,0:T(2,128)(2,1)}), bf16[4,2,40960]{2,1,0:T(2,128)(2,1)S(1)}, u32[]{:S(2)}, u32[]{:S(2)}) async-start(bf16[4,2,40960]{2,1,0:T(2,128)(2,1)} %reshape.43), calls=%async_computation.1 | async-start | bytes 1310720 | tf_op jit(solution)/shard_map/all_to_all | solution.py:45
  195.7 20.6 %all-to-all-start.2 = ((bf16[4,2,40960]{2,1,0:T(2,128)(2,1)}), bf16[4,2,40960]{2,1,0:T(2,128)(2,1)}, u32[]{:S(2)}, u32[]{:S(2)}) async-start(bf16[4,2,40960]{2,1,0:T(2,128)(2,1)} %reshape.45), calls=%async_computation.2 | async-start | bytes 1310720 | tf_op jit(solution)/shard_map/all_to_all | solution.py:48
  202.9 138.3 %all-gather.17.cloned.1.call-start = ((), (), s32[]{:S(2)}) async-start(), calls=%async_computation.12 | async-start | bytes 8192000 | tf_op jit(solution)/shard_map/all_gather | solution.py:91
  227.1 312.3 %reduce-scatter.2.cloned.1.call-start = ((), (), s32[]{:S(2)}) async-start(), calls=%async_computation.13 | async-start | bytes 13107200 | tf_op jit(solution)/shard_map/reduce_scatter | solution.py:95
  283.1 2.9 copy-start
  286.0 3.0 copy-start.1
  298.3 2.9 copy-start
  301.3 3.0 copy-start.1
  313.6 3.0 copy-start
  316.6 3.0 copy-start.1
  328.9 2.9 copy-start
  331.8 3.0 copy-start.1
Sparse Core Ops, SparseCore 0:
  9.8 80.7 all-gather.14
  93.0 50.3 all-gather.6
  145.2 37.8 all-gather.8
  184.8 37.8 all-gather.10
  224.4 37.8 all-gather.12
  263.9 70.5 all-gather.16
  355.2 184.1 reduce-scatter.1
where the time goes:
time: 559 us; the launch traced here: 550 us
  waiting for transfers between devices  192 us (34%)
  local copies, waits for them, and re-layouts  92 us (16%)
  other arithmetic  90.7 us (16%)
  blocking collectives  78.9 us (14%)
  matrix products  68.6 us (12%)
  between operations  14.6 us (3%)
  starting transfers between devices  12.5 us (2%)
    reduce_scatter x1, waiting for transfers between devices, per_device(): lax.psum_scatter(terms.reshape(2, rows_here, width_out).astype(jnp.bfloat...  184 us
    unnamed x11, other arithmetic  85.9 us
    unnamed x41, local copies, waits for them, and re-layouts  48.5 us
    another operation x4, local copies, waits for them, and re-layouts, per_device(): item.reshape(count // 512, 512, heads_here, HEAD_DIM)  28.1 us
    all_to_all x1, blocking collectives, per_device(): lax.all_to_all(key_rows, 'uly', split_axis=2, concat_axis=1, tiled=True)  27.3 us
    all_to_all x1, blocking collectives, per_device(): lax.all_to_all(key_tangent, 'uly', split_axis=2, concat_axis=1, tiled=True)  18.7 us
    dot_general x4, matrix products, block_update(): jnp.einsum('qhd,khd->hqk', query, key, preferred_element_type=jnp.float32)  16.9 us
    all_to_all x1, blocking collectives, per_device(): lax.all_to_all(value_tangent, 'uly', split_axis=2, concat_axis=1, tiled=T...  16.8 us
  transfers between devices with their start and end apart: 9, of which 2 were waited for; matrix products, arithmetic and copies ran while one was open for 42% of the time, Pallas kernels for 0%

commit v1 on v0

v1 whole, which is shorter than its diff:
```python
import jax
import jax.numpy as jnp
from jax import lax
from jax.experimental import pallas as pl
from jax.experimental.pallas import tpu as pltpu
from jax.sharding import PartitionSpec as P

HEAD = 128
STEPS = 5
TOK = 128
SCALE = HEAD ** -0.5
LOG2E = 1.4426950408889634
MESH_IDS = pl.DeviceIdType.MESH
NT = (((1,), (1,)), ((), ()))
KEYS, VALUES, QUERIES = 0, 1, 2
COLUMN_ORDER = (0, 1, 3, 2)


def kernel(
    q_in, k_in, v_in, qt_in, kt_in, vt_in, w_in, out, out_t,
    kvb, qb, ob, ab, wt, acc, stage, wloc,
    a_send, a_recv, z_send, z_recv, c_send, c_recv, r_send, r_recv,
    wz_send, wz_recv, wy_send, wy_recv, wx_send, wx_recv, wd_send, wd_recv,
    l_sem, o_sem,
):
    dp = lax.axis_index("dp")
    uly = lax.axis_index("uly")
    y = lax.axis_index("blk")
    x = lax.rem(dp, 4)
    zl = lax.div(dp, 4)
    zh = lax.div(uly, 2)
    core = lax.rem(uly, 2)
    z = zh * 4 + zl

    def at_z(shift):
        there = lax.rem(z + shift + 8, 8)
        return {
            "dp": lax.rem(there, 4) * 4 + x,
            "uly": lax.div(there, 4) * 2 + core,
            "blk": y,
        }

    def at_y(shift):
        return {"dp": dp, "uly": uly, "blk": lax.rem(y + shift + 4, 4)}

    def at_x(shift):
        return {"dp": zl * 4 + lax.rem(x + shift + 4, 4), "uly": uly, "blk": y}

    other_core = {"dp": dp, "uly": zh * 2 + 1 - core, "blk": y}

    def remote(src, dst, send, recv, where):
        return pltpu.make_async_remote_copy(
            src_ref=src, dst_ref=dst, send_sem=send, recv_sem=recv,
            device_id=where, device_id_type=MESH_IDS,
        )

    def await_bytes(ref, sem):
        pltpu.make_async_copy(ref, ref, sem).wait()

    load_w = pltpu.make_async_copy(w_in, wloc, l_sem)
    load_w.start()

    partners = [at_y(1), at_y(2), at_y(3), at_x(1), at_x(-1), at_z(1), at_z(-1), at_z(4), other_core]
    barrier = pltpu.get_barrier_semaphore()
    for where in partners:
        pl.semaphore_signal(barrier, inc=1, device_id=where, device_id_type=MESH_IDS)
    pl.semaphore_wait(barrier, len(partners))

    pairs = ((k_in, kt_in), (v_in, vt_in), (q_in, qt_in))

    def landing(step, pair):
        if pair == QUERIES:
            return qb.at[step]
        return kvb.at[step, 0, 0, pl.ds(2 * pair, 2)]

    def heads_start(step, pair):
        land = landing(step, pair)
        for item in range(2):
            source = pairs[pair][item]
            for shift in (2, 1, 3, 0):
                owner = lax.rem(y + shift, 4)
                columns = pl.ds(pl.multiple_of(owner * (STEPS * HEAD) + step * HEAD, HEAD), HEAD)
                src = source.at[0, :, columns]
                if shift == 0:
                    pltpu.make_async_copy(src, land.at[item, 0], a_recv.at[step, pair]).start()
                else:
                    remote(src, land.at[item, shift], a_send.at[step, pair], a_recv.at[step, pair], at_y(shift)).start()

    def heads_wait(step, pair):
        await_bytes(landing(step, pair), a_recv.at[step, pair])

    def heads_sent(step, pair):
        if pair == QUERIES:
            await_bytes(qb.at[step, :, pl.ds(1, 3)], a_send.at[step, pair])
        else:
            await_bytes(kvb.at[step, 0, 0, pl.ds(2 * pair, 2), pl.ds(1, 3)], a_send.at[step, pair])

    def quarter(step, pair, rz, rc):
        return kvb.at[step, rz, rc, pl.ds(2 * pair, 2)]

    def z_copy(step, pair):
        half = 2 * step + pair
        return remote(quarter(step, pair, 0, 0), quarter(step, pair, 1, 0), z_send.at[half], z_recv.at[half], at_z(4))

    def core_copy(step, pair, rz):
        half = 2 * step + pair
        return remote(
            quarter(step, pair, rz, 0), quarter(step, pair, rz, 1),
            c_send.at[half, rz], c_recv.at[half, rz], other_core,
        )

    def spread_own(step):
        for pair in (KEYS, VALUES):
            heads_wait(step, pair)
            z_copy(step, pair).start()
            core_copy(step, pair, 0).start()

    def w_block(shift, rows):
        there = lax.rem(z + shift + 8, 8)
        return wt.at[lax.div(there, 4) * 2 + core, y, lax.rem(there, 4), x, rows]

    def wz_copy(ring, side):
        rows = pl.ds(0, 80)
        if ring == 3:
            rows = pl.ds(0, 48) if side == 1 else pl.ds(48, 32)
        src = w_block(-side * ring, rows)
        way = (side + 1) // 2
        return remote(src, src, wz_send.at[ring, way], wz_recv.at[ring, way], at_z(side))

    def group(rel_zh):
        return lax.rem(zh + rel_zh, 2) * 2 + core

    def wy_copy(rel_zh, ring, side):
        way = (side + 1) // 2
        if ring == 0:
            src = wt.at[group(rel_zh), y, :, x]
        else:
            there = lax.rem(y - side + 4, 4)
            src = wt.at[group(rel_zh), there, pl.ds(0, 2) if side == 1 else pl.ds(2, 2), x]
        return remote(src, src, wy_send.at[rel_zh, ring, way], wy_recv.at[rel_zh, ring, way], at_y(side))

    def unit_columns(unit):
        return lax.rem(y + COLUMN_ORDER[unit // 2], 4)

    def wx_copy(unit, ring, side):
        way = (side + 1) // 2
        if ring == 0:
            src = wt.at[group(unit % 2), unit_columns(unit), :, x]
        else:
            there = lax.rem(x - side + 4, 4)
            src = wt.at[group(unit % 2), unit_columns(unit), pl.ds(0, 2) if side == 1 else pl.ds(2, 2), there]
        return remote(src, src, wx_send.at[unit, ring, way], wx_recv.at[unit, ring, way], at_x(side))

    def wd_copy(unit):
        src = wt.at[group(unit % 2), unit_columns(unit)]
        return remote(src, src, wd_send.at[unit], wd_recv.at[unit], other_core)

    def both(make, *key):
        return [make(*key, side) for side in (1, -1)]

    def start(copies):
        for copy in copies:
            copy.start()

    def recv(copies):
        for copy in copies:
            copy.wait_recv()

    def recv_other_core(unit):
        src = wt.at[lax.rem(zh + unit % 2, 2) * 2 + 1 - core, unit_columns(unit)]
        await_bytes(src, wd_recv.at[unit])

    def attention(step):
        def block(index, carry):
            rows = pl.ds(index * 2, 2)
            query = qb[step, 0, rows].reshape(2 * TOK, HEAD)
            query_tan = qb[step, 1, rows].reshape(2 * TOK, HEAD)
            key, key_tan, value, value_tan = (
                kvb[step, :, :, item].reshape(16 * TOK, HEAD) for item in range(4)
            )
            scores = lax.dot_general(query, key, NT, preferred_element_type=jnp.float32)
            top = jnp.max(scores, axis=1, keepdims=True)
            weights = jnp.exp2((scores - top) * (SCALE * LOG2E))
            score_tan = lax.dot_general(
                jnp.concatenate([query_tan, query], axis=1),
                jnp.concatenate([key, key_tan], axis=1),
                NT, preferred_element_type=jnp.float32,
            )
            moved = weights * score_tan
            total = jnp.sum(weights, axis=1, keepdims=True)
            spread = jnp.sum(moved, axis=1, keepdims=True) * SCALE
            low = weights.astype(jnp.bfloat16)
            moved_low = moved.astype(jnp.bfloat16)
            sums = jnp.dot(low, jnp.concatenate([value, value_tan], axis=1), preferred_element_type=jnp.float32)
            plain = sums[:, :HEAD]
            carried = sums[:, HEAD:] + SCALE * jnp.dot(moved_low, value, preferred_element_type=jnp.float32)
            attended = plain / total
            attended_tan = (carried - (spread / total) * plain) / total
            ob[step, rows, 0] = attended.astype(jnp.bfloat16).reshape(2, TOK, HEAD)
            ob[step, rows, 1] = attended_tan.astype(jnp.bfloat16).reshape(2, TOK, HEAD)
            return carry

        lax.fori_loop(0, 2, block, 0)

    def home_copy(step, shift):
        return remote(ob.at[step, shift], ab.at[step, shift], r_send.at[step], r_recv.at[step], at_y(-shift))

    def home_start(step):
        start([home_copy(step, shift) for shift in (2, 1, 3)])

    def home_wait(step):
        await_bytes(ab.at[step, pl.ds(1, 3)], r_recv.at[step])

    def product(block, step):
        left = [ob[step, 0]] + [ab[step, shift] for shift in range(1, 4)]
        left = jnp.concatenate([item.reshape(2 * TOK, HEAD) for item in left], axis=1)
        lanes = pl.ds(pl.multiple_of(step * HEAD, HEAD), HEAD)
        right = jnp.concatenate(
            [wt[lax.rem(y + shift, 4), block, :, :, :, lanes].reshape(1280, HEAD) for shift in range(4)], axis=1
        )
        return lax.dot_general(left, right, NT, preferred_element_type=jnp.float32)

    def project(first, blocks, start_step, steps):
        def one(index, carry):
            rel = first + lax.div(index, steps)
            step = start_step + lax.rem(index, steps)
            shift = rel + lax.div(rel, 2) * (5 - 2 * rel)
            block = lax.rem(y + shift, 4)
            acc[block] += product(block, step)
            return carry

        lax.fori_loop(0, blocks * steps, one, 0)

    def out_copies(block):
        columns = pl.ds(pl.multiple_of(block * 1280, 1280), 1280)
        return [
            pltpu.make_async_copy(stage.at[block, pl.ds(item * TOK, TOK)], ref.at[0, :, columns], o_sem.at[block, item])
            for item, ref in enumerate((out, out_t))
        ]

    for pair in (KEYS, VALUES, QUERIES):
        heads_start(0, pair)
    load_w.wait()
    unit = (
        lax.broadcasted_iota(jnp.int32, (80, 80), 0) == lax.broadcasted_iota(jnp.int32, (80, 80), 1)
    ).astype(jnp.bfloat16)
    turned = lax.dot_general(unit, wloc[...], NT, preferred_element_type=jnp.float32)
    wt[uly, y, zl, x] = turned.astype(jnp.bfloat16)
    start(both(wz_copy, 0))
    spread_own(0)
    for pair in (KEYS, VALUES, QUERIES):
        heads_start(1, pair)
    acc[...] = jnp.zeros_like(acc)
    for ring in range(1, 4):
        recv(both(wz_copy, ring - 1))
        start(both(wz_copy, ring))
    recv(both(wz_copy, 3))
    for rel_zh in range(2):
        start(both(wx_copy, rel_zh, 0))
        start(both(wy_copy, rel_zh, 0))
    for step in range(1, STEPS):
        spread_own(step)
        if step + 1 < STEPS:
            for pair in (KEYS, VALUES, QUERIES):
                heads_start(step + 1, pair)

    for half in range(2 * STEPS):
        step, pair = half // 2, half % 2
        if half == 1:
            for rel_zh in range(2):
                recv(both(wy_copy, rel_zh, 0))
                start(both(wy_copy, rel_zh, 1))
            start(both(wx_copy, 2, 0))
            start(both(wx_copy, 3, 0))
        if 2 <= half <= 5:
            if half == 4:
                for rel_zh in range(2):
                    recv(both(wy_copy, rel_zh, 1))
            start(both(wx_copy, half + 2, 0))
        if half < 8:
            recv(both(wx_copy, half, 0))
            start(both(wx_copy, half, 1))
        if 1 <= half <= 8:
            recv(both(wx_copy, half - 1, 1))
            wd_copy(half - 1).start()
        if 2 <= half:
            recv_other_core(half - 2)
        if half == 8:
            home_wait(0)
            home_wait(1)
            home_wait(2)
            project(0, 3, 0, 3)
        if half == 9:
            home_wait(3)
            project(0, 3, 3, 1)
            project(3, 1, 0, 4)
            for other in range(STEPS):
                for kind in range(3):
                    heads_sent(other, kind)
                if other < 4:
                    await_bytes(ob.at[other, pl.ds(1, 3)], r_send.at[other])
            for other in range(8):
                for ring in range(2):
                    for copy in both(wx_copy, other, ring):
                        copy.wait_send()
                wd_copy(other).wait_send()
            for ring in range(4):
                for copy in both(wz_copy, ring):
                    copy.wait_send()
            for rel_zh in range(2):
                for ring in range(2):
                    for copy in both(wy_copy, rel_zh, ring):
                        copy.wait_send()
            for other in range(2 * STEPS):
                core_copy(other // 2, other % 2, 0).wait_send()
                if other < 9:
                    core_copy(other // 2, other % 2, 1).wait_send()
                    z_copy(other // 2, other % 2).wait_send()
        z_copy(step, pair).wait_recv()
        core_copy(step, pair, 1).start()
        if pair == VALUES:
            heads_wait(step, QUERIES)
            for kind in (KEYS, VALUES):
                for rz in range(2):
                    core_copy(step, kind, rz).wait_recv()
            attention(step)
            home_start(step)

    last = STEPS - 1
    home_wait(last)

    def finish(block, carry):
        stage[block] = (acc[block] + product(block, last)).astype(jnp.bfloat16)
        start(out_copies(block))
        return carry

    lax.fori_loop(0, 4, finish, 0)
    z_copy(last, VALUES).wait_send()
    core_copy(last, VALUES, 1).wait_send()
    await_bytes(ob.at[last, pl.ds(1, 3)], r_send.at[last])

    def drain(block, carry):
        for copy in out_copies(block):
            copy.wait()
        return carry

    lax.fori_loop(0, 4, drain, 0)


def per_device(*arrays):
    dma = pltpu.SemaphoreType.DMA
    low = jnp.bfloat16
    result = jax.ShapeDtypeStruct((1, TOK, 5120), low)
    anywhere = pl.BlockSpec(memory_space=pl.ANY)
    return pl.pallas_call(
        kernel,
        out_shape=(result, result),
        in_specs=[anywhere] * 7,
        out_specs=(anywhere, anywhere),
        scratch_shapes=[
            pltpu.VMEM((STEPS, 2, 2, 4, 4, TOK, HEAD), low),
            pltpu.VMEM((STEPS, 2, 4, TOK, HEAD), low),
            pltpu.VMEM((STEPS, 4, 2, TOK, HEAD), low),
            pltpu.VMEM((STEPS, 4, 2, TOK, HEAD), low),
            pltpu.VMEM((4, 4, 4, 4, 80, 640), low),
            pltpu.VMEM((4, 2 * TOK, 1280), jnp.float32),
            pltpu.VMEM((4, 2 * TOK, 1280), low),
            pltpu.VMEM((640, 80), low),
            dma((STEPS, 3)), dma((STEPS, 3)),
            dma((2 * STEPS,)), dma((2 * STEPS,)),
            dma((2 * STEPS, 2)), dma((2 * STEPS, 2)),
            dma((STEPS,)), dma((STEPS,)),
            dma((4, 2)), dma((4, 2)),
            dma((2, 2, 2)), dma((2, 2, 2)),
            dma((8, 2, 2)), dma((8, 2, 2)),
            dma((8,)), dma((8,)),
            dma, dma((4, 2)),
        ],
        compiler_params=pltpu.CompilerParams(
            collective_id=0, has_side_effects=True, vmem_limit_bytes=64 * 1024 * 1024
        ),
    )(*arrays)


def solution(mesh):
    rows = P("dp", ("uly", "blk"), None)
    return jax.shard_map(
        per_device,
        mesh=mesh,
        in_specs=(rows,) * 6 + (P("uly", ("blk", "dp")),),
        out_specs=(rows, rows),
        check_vma=False,
    )
```

time: 559 us -> 210 us (0.38); the launches traced: 550 us -> 210 us
  Pallas kernels: 0 us -> 204 us
  waiting for transfers between devices: 192 us -> 0 us
  other arithmetic: 90.7 us -> 0 us
  local copies, waits for them, and re-layouts: 92 us -> 5.32 us
  blocking collectives: 78.9 us -> 0 us
  matrix products: 68.6 us -> 0 us
  between operations: 14.6 us -> 0.65 us
  starting transfers between devices: 12.5 us -> 0 us
    pallas_call x0 -> x1, Pallas kernels: none -> 204 us  [per_device(): pl.pallas_call(kernel, out_shape=(result, result), in_specs=[anywhere] *...]
    reduce_scatter x1 -> x0, waiting for transfers between devices: 184 us -> none  [per_device(): lax.psum_scatter(terms.reshape(2, rows_here, width_out).astype(jnp.bfloat...]
    unnamed x11 -> x0, other arithmetic: 85.9 us -> none
    all_to_all x4 -> x0, blocking collectives: 78.9 us -> none  [the longest x1 27.3 us: per_device(): lax.all_to_all(key_rows, 'uly', split_axis=2, concat_axis=1, tiled=True)]
    dot_general x25 -> x0, matrix products: 68.6 us -> none  [the longest x4 16.9 us: block_update(): jnp.einsum('qhd,khd->hqk', query, key, preferred_element_type=jnp.float32)]
    unnamed x41 -> x5, local copies, waits for them, and re-layouts: 48.5 us -> 5.32 us
    another operation x6 -> x0, local copies, waits for them, and re-layouts: 31.4 us -> none  [the longest x4 28.1 us: per_device(): item.reshape(count // 512, 512, heads_here, HEAD_DIM)]
    all_to_all x2 -> x0, starting transfers between devices: 11.7 us -> none  [the longest x1 7.2 us: per_device(): lax.all_to_all(query_tangent, 'uly', split_axis=2, concat_axis=1, tiled=T...]
  transfers between devices with their start and end apart: 9 -> 0, of which waited for: 2 -> 0; matrix products, arithmetic and copies ran while one was open for 42% -> 0% of each run, Pallas kernels for 0% -> 0%
where the time goes in v1:
time: 210 us
  Pallas kernels  204 us (97%)
  local copies, waits for them, and re-layouts  5.32 us (3%)
    pallas_call x1, Pallas kernels, per_device(): pl.pallas_call(kernel, out_shape=(result, result), in_specs=[anywhere] *...  204 us
    unnamed x5, local copies, waits for them, and re-layouts  5.32 us

profile of v1, /device:TPU:1, one launch (start us, length us, event | category | flops | bytes accessed | tf_op | source)
XLA Modules:
  0.0 209.9 jit_solution(5211596565489347803)
XLA Ops:
  0.6 1.7 copy.9.w_in
  2.3 203.9 %shard_map.86 = (bf16[1,128,5120]{2,1,0:T(8,128)(2,1)}, bf16[1,128,5120]{2,1,0:T(8,128)(2,1)}) custom-call(bf16[1,128,2560]{2,1,0:T(8,128)(2,1)} %q_in.1, bf16[1,128,2560]{2,1,0:T(8,128)(2,1)} %k_in.1, bf16[1,128,2560]{2,1,0:T(8,128)(2,1)} %v_in.1, bf16[1,128,2560]{2,1,0:T(8,128)(2,1)} %qt_in.1, bf16[1,128,2560]{2,1,0:T(8,128)(2,1)} %kt_in.1, ...), custom_call_target="tpu_custom_call" | custom-call | tf_op jit(solution)/shard_map/pallas_call | solution.py:355
  206.3 0.0 copy-start
  206.3 2.6 %copy.12 = bf16[1,128,5120]{2,1,0:T(8,128)(2,1)} copy(bf16[1,128,5120]{2,1,0:T(8,128)(2,1)} %get-tuple-element.4) | data formatting | bytes 2621440
  208.8 0.0 copy-done
  208.8 1.1 copy.13
Async XLA Ops:
  206.3 2.6 %copy-start = (bf16[1,128,5120]{2,1,0:T(8,128)(2,1)S(1)}, bf16[1,128,5120]{2,1,0:T(8,128)(2,1)}, u32[]{:S(2)}) copy-start(bf16[1,128,5120]{2,1,0:T(8,128)(2,1)} %get-tuple-element.5) | copy-start | bytes 3932164

commit v2 on v1

v2 whole, which is shorter than its diff:
```python
import jax
import jax.numpy as jnp
from jax import lax
from jax.experimental import pallas as pl
from jax.experimental.pallas import tpu as pltpu
from jax.sharding import PartitionSpec as P

HEAD = 128
STEPS = 5
TOK = 128
SCALE = HEAD ** -0.5
LOG2E = 1.4426950408889634
MESH_IDS = pl.DeviceIdType.MESH
NT = (((1,), (1,)), ((), ()))
KEYS, VALUES, QUERIES = 0, 1, 2
COLUMN_ORDER = (0, 1, 3, 2)


def kernel(
    q_in, k_in, v_in, qt_in, kt_in, vt_in, w_in, out, out_t, relay,
    kvb, qb, ob, ab, wt, acc, stage, low_ref, moved_ref, total_ref, spread_ref,
    a_send, a_recv, z_send, z_recv, c_send, c_recv, r_send, r_recv,
    wz_send, wz_recv, wy_send, wy_recv, wx_send, wx_recv, wd_send, wd_recv,
    xb_send, xb_recv, yb_send, yb_recv, db_send, db_recv,
    l_sem, o_sem,
):
    dp = lax.axis_index("dp")
    uly = lax.axis_index("uly")
    y = lax.axis_index("blk")
    x = lax.rem(dp, 4)
    zl = lax.div(dp, 4)
    zh = lax.div(uly, 2)
    core = lax.rem(uly, 2)
    z = zh * 4 + zl

    def at_z(shift):
        there = lax.rem(z + shift + 8, 8)
        return {
            "dp": lax.rem(there, 4) * 4 + x,
            "uly": lax.div(there, 4) * 2 + core,
            "blk": y,
        }

    def at_y(shift):
        return {"dp": dp, "uly": uly, "blk": lax.rem(y + shift + 4, 4)}

    def at_x(shift):
        return {"dp": zl * 4 + lax.rem(x + shift + 4, 4), "uly": uly, "blk": y}

    other_core = {"dp": dp, "uly": zh * 2 + 1 - core, "blk": y}

    def remote(src, dst, send, recv, where):
        return pltpu.make_async_remote_copy(
            src_ref=src, dst_ref=dst, send_sem=send, recv_sem=recv,
            device_id=where, device_id_type=MESH_IDS,
        )

    def await_bytes(ref, sem):
        pltpu.make_async_copy(ref, ref, sem).wait()

    load_w = pltpu.make_async_copy(w_in, wt.at[uly, y, zl, x], l_sem)
    load_w.start()

    partners = [at_y(1), at_y(2), at_y(3), at_x(1), at_x(-1), at_z(1), at_z(-1), other_core]
    barrier = pltpu.get_barrier_semaphore()
    for where in partners:
        pl.semaphore_signal(barrier, inc=1, device_id=where, device_id_type=MESH_IDS)
    pl.semaphore_wait(barrier, len(partners))

    pairs = ((k_in, kt_in), (v_in, vt_in), (q_in, qt_in))

    def landing(step, pair):
        if pair == QUERIES:
            return qb.at[step]
        return kvb.at[step, 0, 0, pl.ds(2 * pair, 2)]

    def heads_start(step, pair):
        land = landing(step, pair)
        for item in range(2):
            source = pairs[pair][item]
            for shift in (2, 1, 3, 0):
                owner = lax.rem(y + shift, 4)
                columns = pl.ds(pl.multiple_of(owner * (STEPS * HEAD) + step * HEAD, HEAD), HEAD)
                src = source.at[0, :, columns]
                if shift == 0:
                    pltpu.make_async_copy(src, land.at[item, 0], a_recv.at[step, pair]).start()
                else:
                    remote(src, land.at[item, shift], a_send.at[step, pair], a_recv.at[step, pair], at_y(shift)).start()

    def heads_wait(step, pair):
        await_bytes(landing(step, pair), a_recv.at[step, pair])

    def heads_sent(step, pair):
        if pair == QUERIES:
            await_bytes(qb.at[step, :, pl.ds(1, 3)], a_send.at[step, pair])
        else:
            await_bytes(kvb.at[step, 0, 0, pl.ds(2 * pair, 2), pl.ds(1, 3)], a_send.at[step, pair])

    def quarter(step, pair, rz, rc):
        return kvb.at[step, rz, rc, pl.ds(2 * pair, 2)]

    def z_copy(half, hop, way):
        step, pair = half // 2, half % 2
        src = kvb.at[step, 0, 0, 2 * pair + way] if hop == 1 else relay.at[half, hop - 2, way]
        dst = kvb.at[step, 1, 0, 2 * pair + way] if hop == 4 else relay.at[half, hop - 1, way]
        return remote(
            src, dst, z_send.at[half, hop - 1, way], z_recv.at[half, hop - 1, way], at_z(1 - 2 * way)
        )

    def z_copies(half, hop):
        return [z_copy(half, hop, way) for way in range(2)]

    def core_copy(step, pair, rz):
        half = 2 * step + pair
        return remote(
            quarter(step, pair, rz, 0), quarter(step, pair, rz, 1),
            c_send.at[half, rz], c_recv.at[half, rz], other_core,
        )

    def z_round(turn):
        for hop in (3, 2, 1):
            if 0 <= turn - hop < 2 * STEPS:
                recv(z_copies(turn - hop, hop))
                start(z_copies(turn - hop, hop + 1))
        if turn < 2 * STEPS:
            step, pair = turn // 2, turn % 2
            heads_wait(step, pair)
            start(z_copies(turn, 1))
            core_copy(step, pair, 0).start()

    def w_block(shift, rows):
        there = lax.rem(z + shift + 8, 8)
        return wt.at[lax.div(there, 4) * 2 + core, y, lax.rem(there, 4), x, rows]

    def wz_copy(ring, side):
        rows = pl.ds(0, 80)
        if ring == 3:
            rows = pl.ds(0, 48) if side == 1 else pl.ds(48, 32)
        dst = w_block(-side * ring, rows)
        way = (side + 1) // 2
        src = w_in if ring == 0 else dst
        return remote(src, dst, wz_send.at[ring, way], wz_recv.at[ring, way], at_z(side))

    def group(rel_zh):
        return lax.rem(zh + rel_zh, 2) * 2 + core

    first, rest = pl.ds(0, 3), 3

    def wy_copy(rel_zh, ring, side):
        way = (side + 1) // 2
        there = y if ring == 0 else lax.rem(y - side + 4, 4)
        src = wt.at[group(rel_zh), there, first, x]
        return remote(src, src, wy_send.at[rel_zh, ring, way], wy_recv.at[rel_zh, ring, way], at_y(side))

    def xb_copy(rel_zh, ring, side):
        way = (side + 1) // 2
        there = x if ring == 0 else lax.rem(x - side + 4, 4)
        src = wt.at[group(rel_zh), y, rest, there]
        return remote(src, src, xb_send.at[rel_zh, ring, way], xb_recv.at[rel_zh, ring, way], at_x(side))

    def yb_copy(rel_zh, ring, side):
        way = (side + 1) // 2
        there = y if ring == 0 else lax.rem(y - side + 4, 4)
        src = wt.at[group(rel_zh), there, rest]
        return remote(src, src, yb_send.at[rel_zh, ring, way], yb_recv.at[rel_zh, ring, way], at_y(side))

    def unit_columns(unit):
        return lax.rem(y + COLUMN_ORDER[unit // 2], 4)

    def wx_copy(unit, ring, side):
        way = (side + 1) // 2
        there = x if ring == 0 else lax.rem(x - side + 4, 4)
        src = wt.at[group(unit % 2), unit_columns(unit), first, there]
        return remote(src, src, wx_send.at[unit, ring, way], wx_recv.at[unit, ring, way], at_x(side))

    def wd_copy(unit):
        src = wt.at[group(unit % 2), unit_columns(unit), first]
        return remote(src, src, wd_send.at[unit], wd_recv.at[unit], other_core)

    def db_copy(unit):
        src = wt.at[group(unit % 2), unit_columns(unit), rest]
        return remote(src, src, db_send.at[unit], db_recv.at[unit], other_core)

    def both(make, *key):
        return [make(*key, side) for side in (1, -1)]

    def ring_of(make, index, ring):
        if ring == 0:
            return both(make, index, 0)
        return [make(index, 1, 1 if index % 2 == 0 else -1)]

    def start(copies):
        for copy in copies:
            copy.start()

    def recv(copies):
        for copy in copies:
            copy.wait_recv()

    def recv_other_core(unit):
        other_group = lax.rem(zh + unit % 2, 2) * 2 + 1 - core
        await_bytes(wt.at[other_group, unit_columns(unit), first], wd_recv.at[unit])

    def recv_other_rest(unit):
        other_group = lax.rem(zh + unit % 2, 2) * 2 + 1 - core
        await_bytes(wt.at[other_group, unit_columns(unit), rest], db_recv.at[unit])

    def weigh(step):
        def block(index, carry):
            rows = pl.ds(index * 2, 2)
            query = qb[step, 0, rows].reshape(2 * TOK, HEAD)
            query_tan = qb[step, 1, rows].reshape(2 * TOK, HEAD)
            key, key_tan = (kvb[step, :, :, item].reshape(16 * TOK, HEAD) for item in range(2))
            scores = lax.dot_general(query, key, NT, preferred_element_type=jnp.float32)
            top = jnp.max(scores, axis=1, keepdims=True)
            weights = jnp.exp2((scores - top) * (SCALE * LOG2E))
            score_tan = lax.dot_general(
                jnp.concatenate([query_tan, query], axis=1),
                jnp.concatenate([key, key_tan], axis=1),
                NT, preferred_element_type=jnp.float32,
            )
            moved = weights * score_tan
            total_ref[index] = jnp.sum(weights, axis=1, keepdims=True)
            spread_ref[index] = jnp.sum(moved, axis=1, keepdims=True) * SCALE
            low_ref[index] = weights.astype(jnp.bfloat16)
            moved_ref[index] = moved.astype(jnp.bfloat16)
            return carry

        lax.fori_loop(0, 2, block, 0)

    def attend(step):
        def block(index, carry):
            rows = pl.ds(index * 2, 2)
            value, value_tan = (kvb[step, :, :, item].reshape(16 * TOK, HEAD) for item in range(2, 4))
            total = total_ref[index]
            sums = jnp.dot(
                low_ref[index], jnp.concatenate([value, value_tan], axis=1), preferred_element_type=jnp.float32
            )
            plain = sums[:, :HEAD]
            carried = sums[:, HEAD:] + SCALE * jnp.dot(moved_ref[index], value, preferred_element_type=jnp.float32)
            attended = plain / total
            attended_tan = (carried - (spread_ref[index] / total) * plain) / total
            ob[step, rows, 0] = attended.astype(jnp.bfloat16).reshape(2, TOK, HEAD)
            ob[step, rows, 1] = attended_tan.astype(jnp.bfloat16).reshape(2, TOK, HEAD)
            return carry

        lax.fori_loop(0, 2, block, 0)

    def home_copy(step, shift):
        return remote(ob.at[step, shift], ab.at[step, shift], r_send.at[step], r_recv.at[step], at_y(-shift))

    def home_start(step):
        start([home_copy(step, shift) for shift in (2, 1, 3)])

    def home_wait(step):
        await_bytes(ab.at[step, pl.ds(1, 3)], r_recv.at[step])

    def product(block, step):
        left = [ob[step, 0]] + [ab[step, shift] for shift in range(1, 4)]
        left = jnp.concatenate([item.reshape(2 * TOK, HEAD) for item in left], axis=1)
        lanes = pl.ds(pl.multiple_of(step * HEAD, HEAD), HEAD)
        right = jnp.concatenate(
            [wt[lax.rem(y + shift, 4), block, :, :, :, lanes].reshape(1280, HEAD) for shift in range(4)], axis=1
        )
        return lax.dot_general(left, right, NT, preferred_element_type=jnp.float32)

    def project(first, blocks, start_step, steps):
        def one(index, carry):
            rel = first + lax.div(index, steps)
            step = start_step + lax.rem(index, steps)
            shift = rel + lax.div(rel, 2) * (5 - 2 * rel)
            block = lax.rem(y + shift, 4)
            acc[block] += product(block, step)
            return carry

        lax.fori_loop(0, blocks * steps, one, 0)

    def out_copies(block):
        columns = pl.ds(pl.multiple_of(block * 1280, 1280), 1280)
        return [
            pltpu.make_async_copy(stage.at[block, pl.ds(item * TOK, TOK)], ref.at[0, :, columns], o_sem.at[block, item])
            for item, ref in enumerate((out, out_t))
        ]

    def heads_of(step):
        for pair in (KEYS, VALUES, QUERIES):
            heads_start(step, pair)

    def sends_done():
        for step in range(STEPS):
            for kind in range(3):
                heads_sent(step, kind)
            if step < 4:
                await_bytes(ob.at[step, pl.ds(1, 3)], r_send.at[step])
        copies = []
        for unit in range(8):
            for ring in range(2):
                copies += ring_of(wx_copy, unit, ring)
            copies += [wd_copy(unit), db_copy(unit)]
        for ring in range(4):
            copies += both(wz_copy, ring)
        for rel_zh in range(2):
            for ring in range(2):
                for make in (wy_copy, xb_copy, yb_copy):
                    copies += ring_of(make, rel_zh, ring)
        for half in range(2 * STEPS):
            copies.append(core_copy(half // 2, half % 2, 0))
            for hop in range(1, 5):
                copies += z_copies(half, hop)
            if half < 9:
                copies.append(core_copy(half // 2, half % 2, 1))
        for copy in copies:
            copy.wait_send()

    def x_forward(unit):
        recv(ring_of(wx_copy, unit, 0))
        start(ring_of(wx_copy, unit, 1))
        if 2 <= unit + 2 <= 7:
            start(ring_of(wx_copy, unit + 2, 0))

    def x_done(unit):
        recv(ring_of(wx_copy, unit, 1))
        wd_copy(unit).start()

    def z_arrived(half):
        step, pair = half // 2, half % 2
        recv(z_copies(half, 4))
        core_copy(step, pair, 1).start()
        if pair == KEYS:
            heads_wait(step, QUERIES)
        core_copy(step, pair, 0).wait_recv()
        core_copy(step, pair, 1).wait_recv()
        if pair == KEYS:
            weigh(step)
        else:
            attend(step)
            home_start(step)

    def y_ring(make, ring):
        for rel_zh in range(2):
            start(ring_of(make, rel_zh, ring))

    def y_recv(make, ring):
        for rel_zh in range(2):
            recv(ring_of(make, rel_zh, ring))

    start(both(wz_copy, 0))
    heads_of(0)
    acc[...] = jnp.zeros_like(acc)
    heads_of(1)
    recv(both(wz_copy, 0))
    start(both(wz_copy, 1))
    z_round(0)
    recv(both(wz_copy, 1))
    start(both(wz_copy, 2))
    z_round(1)
    recv(both(wz_copy, 2))
    start(both(wz_copy, 3))
    z_round(2)
    recv(both(wz_copy, 3))
    load_w.wait()
    start(ring_of(wx_copy, 0, 0))
    y_ring(wy_copy, 0)
    y_ring(xb_copy, 0)
    start(ring_of(wx_copy, 1, 0))
    heads_of(2)
    z_round(3)
    y_recv(wy_copy, 0)
    x_forward(0)
    heads_of(3)
    y_ring(wy_copy, 1)
    z_round(4)
    y_recv(xb_copy, 0)
    y_ring(xb_copy, 1)
    x_forward(1)
    x_done(0)
    z_arrived(0)
    z_round(5)
    x_forward(2)
    x_done(1)
    heads_of(4)
    y_recv(xb_copy, 1)
    y_recv(wy_copy, 1)
    db_copy(0).start()
    db_copy(1).start()
    z_arrived(1)
    z_round(6)
    y_ring(yb_copy, 0)
    x_forward(3)
    x_done(2)
    z_arrived(2)
    z_round(7)
    x_forward(4)
    x_done(3)
    z_arrived(3)
    z_round(8)
    x_forward(5)
    x_done(4)
    y_recv(yb_copy, 0)
    y_ring(yb_copy, 1)
    for unit in range(2, 6):
        db_copy(unit).start()
    z_arrived(4)
    z_round(9)
    x_forward(6)
    x_done(5)
    z_arrived(5)
    z_round(10)
    x_forward(7)
    x_done(6)
    y_recv(yb_copy, 1)
    db_copy(6).start()
    db_copy(7).start()
    for unit in range(6):
        recv_other_core(unit)
        recv_other_rest(unit)
    for step in range(2):
        home_wait(step)
    project(0, 3, 0, 2)
    z_arrived(6)
    z_round(11)
    x_done(7)
    home_wait(2)
    project(0, 3, 2, 1)
    z_arrived(7)
    z_round(12)
    for unit in range(6, 8):
        recv_other_core(unit)
        recv_other_rest(unit)
    project(3, 1, 0, 3)
    z_arrived(8)
    home_wait(3)
    project(0, 4, 3, 1)
    sends_done()
    z_arrived(9)

    last = STEPS - 1
    home_wait(last)

    def finish(block, carry):
        stage[block] = (acc[block] + product(block, last)).astype(jnp.bfloat16)
        start(out_copies(block))
        return carry

    lax.fori_loop(0, 4, finish, 0)
    core_copy(last, VALUES, 1).wait_send()
    await_bytes(ob.at[last, pl.ds(1, 3)], r_send.at[last])

    def drain(block, carry):
        for copy in out_copies(block):
            copy.wait()
        return carry

    lax.fori_loop(0, 4, drain, 0)


def per_device(*arrays):
    dma = pltpu.SemaphoreType.DMA
    low = jnp.bfloat16
    result = jax.ShapeDtypeStruct((1, TOK, 5120), low)
    anywhere = pl.BlockSpec(memory_space=pl.ANY)
    return pl.pallas_call(
        kernel,
        out_shape=(result, result, jax.ShapeDtypeStruct((2 * STEPS, 3, 2, 4, TOK, HEAD), low)),
        in_specs=[anywhere] * 7,
        out_specs=(anywhere, anywhere, anywhere),
        scratch_shapes=[
            pltpu.VMEM((STEPS, 2, 2, 4, 4, TOK, HEAD), low),
            pltpu.VMEM((STEPS, 2, 4, TOK, HEAD), low),
            pltpu.VMEM((STEPS, 4, 2, TOK, HEAD), low),
            pltpu.VMEM((STEPS, 4, 2, TOK, HEAD), low),
            pltpu.VMEM((4, 4, 4, 4, 80, 640), low),
            pltpu.VMEM((4, 2 * TOK, 1280), jnp.float32),
            pltpu.VMEM((4, 2 * TOK, 1280), low),
            pltpu.VMEM((2, 2 * TOK, 16 * TOK), low),
            pltpu.VMEM((2, 2 * TOK, 16 * TOK), low),
            pltpu.VMEM((2, 2 * TOK, 1), jnp.float32),
            pltpu.VMEM((2, 2 * TOK, 1), jnp.float32),
            dma((STEPS, 3)), dma((STEPS, 3)),
            dma((2 * STEPS, 4, 2)), dma((2 * STEPS, 4, 2)),
            dma((2 * STEPS, 2)), dma((2 * STEPS, 2)),
            dma((STEPS,)), dma((STEPS,)),
            dma((4, 2)), dma((4, 2)),
            dma((2, 2, 2)), dma((2, 2, 2)),
            dma((8, 2, 2)), dma((8, 2, 2)),
            dma((8,)), dma((8,)),
            dma((2, 2, 2)), dma((2, 2, 2)),
            dma((2, 2, 2)), dma((2, 2, 2)),
            dma((8,)), dma((8,)),
            dma, dma((4, 2)),
        ],
        compiler_params=pltpu.CompilerParams(
            collective_id=0, has_side_effects=True, vmem_limit_bytes=64 * 1024 * 1024
        ),
    )(*arrays[:6], arrays[6].T)[:2]


def solution(mesh):
    rows = P("dp", ("uly", "blk"), None)
    return jax.shard_map(
        per_device,
        mesh=mesh,
        in_specs=(rows,) * 6 + (P("uly", ("blk", "dp")),),
        out_specs=(rows, rows),
        check_vma=False,
    )
```

time: 210 us -> 164 us (0.78)
  Pallas kernels: 204 us -> 159 us
    pallas_call x1, Pallas kernels: 204 us -> 159 us  [per_device(): pl.pallas_call(kernel, out_shape=(result, result, jax.ShapeDtypeStruct((2...]
    unnamed x5 -> x4, local copies, waits for them, and re-layouts: 5.32 us -> 3.62 us
where the time goes in v2:
time: 164 us; the launch traced here: 163 us
  Pallas kernels  159 us (97%)
  local copies, waits for them, and re-layouts  3.62 us (2%)
    pallas_call x1, Pallas kernels, per_device(): pl.pallas_call(kernel, out_shape=(result, result, jax.ShapeDtypeStruct((2...  159 us
    unnamed x4, local copies, waits for them, and re-layouts  3.62 us

profile of v2, /device:TPU:1, one launch (start us, length us, event | category | flops | bytes accessed | tf_op | source)
XLA Modules:
  0.0 163.4 jit_solution(3412459485560329691)
XLA Ops:
  0.6 159.2 %shard_map.86 = (bf16[1,128,5120]{2,1,0:T(8,128)(2,1)}, bf16[1,128,5120]{2,1,0:T(8,128)(2,1)}, bf16[10,3,2,4,128,128]{5,4,3,2,1,0:T(8,128)(2,1)}) custom-call(bf16[1,128,2560]{2,1,0:T(8,128)(2,1)} %q_in.1, bf16[1,128,2560]{2,1,0:T(8,128)(2,1)} %k_in.1, bf16[1,128,2560]{2,1,0:T(8,128)(2,1)} %v_in.1, bf16[1,128,2560]{2,1,0:T(8,128)(2,1)} %qt_in.1, ...), custom_call_target="tpu_custom_call" | custom-call | tf_op jit(solution)/shard_map/pallas_call | solution.py:462
  159.8 0.0 copy-start
  159.8 2.6 %copy.11 = bf16[1,128,5120]{2,1,0:T(8,128)(2,1)} copy(bf16[1,128,5120]{2,1,0:T(8,128)(2,1)} %get-tuple-element.8) | data formatting | bytes 2621440
  162.4 0.0 copy-done
  162.4 1.1 copy.12
Async XLA Ops:
  159.8 2.6 %copy-start = (bf16[1,128,5120]{2,1,0:T(8,128)(2,1)S(1)}, bf16[1,128,5120]{2,1,0:T(8,128)(2,1)}, u32[]{:S(2)}) copy-start(bf16[1,128,5120]{2,1,0:T(8,128)(2,1)} %get-tuple-element.9) | copy-start | bytes 3932164

commit v3 on v2

--- a/solution.py
+++ b/solution.py
@@ -17,8 +17,8 @@
 
 
 def kernel(
-    q_in, k_in, v_in, qt_in, kt_in, vt_in, w_in, out, out_t, relay,
-    kvb, qb, ob, ab, wt, acc, stage, low_ref, moved_ref, total_ref, spread_ref,
+    q_in, k_in, v_in, qt_in, kt_in, vt_in, w_in, out, out_t,
+    relay, kvb, qb, ob, ab, wt, acc, stage, low_ref, moved_ref, total_ref, spread_ref, sums_ref, carry_ref,
     a_send, a_recv, z_send, z_recv, c_send, c_recv, r_send, r_recv,
     wz_send, wz_recv, wy_send, wy_recv, wx_send, wx_recv, wd_send, wd_recv,
     xb_send, xb_recv, yb_send, yb_recv, db_send, db_recv,
@@ -117,16 +117,17 @@
             c_send.at[half, rz], c_recv.at[half, rz], other_core,
         )
 
-    def z_round(turn):
-        for hop in (3, 2, 1):
-            if 0 <= turn - hop < 2 * STEPS:
-                recv(z_copies(turn - hop, hop))
-                start(z_copies(turn - hop, hop + 1))
-        if turn < 2 * STEPS:
-            step, pair = turn // 2, turn % 2
+    def z_own(half):
+        if half < 2 * STEPS:
+            step, pair = half // 2, half % 2
             heads_wait(step, pair)
-            start(z_copies(turn, 1))
+            start(z_copies(half, 1))
             core_copy(step, pair, 0).start()
+
+    def z_forward(half, hop):
+        if 0 <= half < 2 * STEPS:
+            recv(z_copies(half, hop))
+            start(z_copies(half, hop + 1))
 
     def w_block(shift, rows):
         there = lax.rem(z + shift + 8, 8)
@@ -205,52 +206,50 @@
         other_group = lax.rem(zh + unit % 2, 2) * 2 + 1 - core
         await_bytes(wt.at[other_group, unit_columns(unit), rest], db_recv.at[unit])
 
-    def weigh(step):
-        def block(index, carry):
-            rows = pl.ds(index * 2, 2)
-            query = qb[step, 0, rows].reshape(2 * TOK, HEAD)
-            query_tan = qb[step, 1, rows].reshape(2 * TOK, HEAD)
-            key, key_tan = (kvb[step, :, :, item].reshape(16 * TOK, HEAD) for item in range(2))
-            scores = lax.dot_general(query, key, NT, preferred_element_type=jnp.float32)
-            top = jnp.max(scores, axis=1, keepdims=True)
-            weights = jnp.exp2((scores - top) * (SCALE * LOG2E))
-            score_tan = lax.dot_general(
-                jnp.concatenate([query_tan, query], axis=1),
-                jnp.concatenate([key, key_tan], axis=1),
-                NT, preferred_element_type=jnp.float32,
-            )
-            moved = weights * score_tan
-            total_ref[index] = jnp.sum(weights, axis=1, keepdims=True)
-            spread_ref[index] = jnp.sum(moved, axis=1, keepdims=True) * SCALE
-            low_ref[index] = weights.astype(jnp.bfloat16)
-            moved_ref[index] = moved.astype(jnp.bfloat16)
-            return carry
-
-        lax.fori_loop(0, 2, block, 0)
-
-    def attend(step):
-        def block(index, carry):
-            rows = pl.ds(index * 2, 2)
-            value, value_tan = (kvb[step, :, :, item].reshape(16 * TOK, HEAD) for item in range(2, 4))
-            total = total_ref[index]
-            sums = jnp.dot(
-                low_ref[index], jnp.concatenate([value, value_tan], axis=1), preferred_element_type=jnp.float32
-            )
-            plain = sums[:, :HEAD]
-            carried = sums[:, HEAD:] + SCALE * jnp.dot(moved_ref[index], value, preferred_element_type=jnp.float32)
-            attended = plain / total
-            attended_tan = (carried - (spread_ref[index] / total) * plain) / total
-            ob[step, rows, 0] = attended.astype(jnp.bfloat16).reshape(2, TOK, HEAD)
-            ob[step, rows, 1] = attended_tan.astype(jnp.bfloat16).reshape(2, TOK, HEAD)
-            return carry
-
-        lax.fori_loop(0, 2, block, 0)
+    def weigh(step, index):
+        rows = pl.ds(index * 2, 2)
+        query = qb[step, 0, rows].reshape(2 * TOK, HEAD)
+        query_tan = qb[step, 1, rows].reshape(2 * TOK, HEAD)
+        key, key_tan = (kvb[step, :, :, item].reshape(16 * TOK, HEAD) for item in range(2))
+        scores = lax.dot_general(query, key, NT, preferred_element_type=jnp.float32)
+        top = jnp.max(scores, axis=1, keepdims=True)
+        weights = jnp.exp2((scores - top) * (SCALE * LOG2E))
+        score_tan = lax.dot_general(
+            jnp.concatenate([query_tan, query], axis=1),
+            jnp.concatenate([key, key_tan], axis=1),
+            NT, preferred_element_type=jnp.float32,
+        )
+        moved = weights * score_tan
+        total_ref[index] = jnp.sum(weights, axis=1, keepdims=True)
+        spread_ref[index] = jnp.sum(moved, axis=1, keepdims=True) * SCALE
+        low_ref[index] = weights.astype(jnp.bfloat16)
+        moved_ref[index] = moved.astype(jnp.bfloat16)
+
+    def sums_over(step, index, rz, cores):
+        keys = pl.ds((2 * rz + cores.start) * 4 * TOK, cores.size * 4 * TOK)
+        value, value_tan = (
+            kvb[step, rz, cores, item].reshape(cores.size * 4 * TOK, HEAD) for item in range(2, 4)
+        )
+        both_values = jnp.concatenate([value, value_tan], axis=1)
+        sums = jnp.dot(low_ref[index, :, keys], both_values, preferred_element_type=jnp.float32)
+        return sums, jnp.dot(moved_ref[index, :, keys], value, preferred_element_type=jnp.float32)
+
+    def attend(step, index, parts):
+        sums, moved = parts[0]
+        for more, more_moved in parts[1:]:
+            sums, moved = sums + more, moved + more_moved
+        rows = pl.ds(index * 2, 2)
+        total = total_ref[index]
+        plain = sums[:, :HEAD]
+        carried = sums[:, HEAD:] + SCALE * moved
+        attended = plain / total
+        attended_tan = (carried - (spread_ref[index] / total) * plain) / total
+        ob[step, rows, 0] = attended.astype(jnp.bfloat16).reshape(2, TOK, HEAD)
+        ob[step, rows, 1] = attended_tan.astype(jnp.bfloat16).reshape(2, TOK, HEAD)
+        start([home_copy(step, shift) for shift in ((2, 3) if index == 1 else (1,))])
 
     def home_copy(step, shift):
         return remote(ob.at[step, shift], ab.at[step, shift], r_send.at[step], r_recv.at[step], at_y(-shift))
-
-    def home_start(step):
-        start([home_copy(step, shift) for shift in (2, 1, 3)])
 
     def home_wait(step):
         await_bytes(ab.at[step, pl.ds(1, 3)], r_recv.at[step])
@@ -282,15 +281,11 @@
             for item, ref in enumerate((out, out_t))
         ]
 
-    def heads_of(step):
-        for pair in (KEYS, VALUES, QUERIES):
-            heads_start(step, pair)
-
     def sends_done():
         for step in range(STEPS):
             for kind in range(3):
                 heads_sent(step, kind)
-            if step < 4:
+            if step < 3:
                 await_bytes(ob.at[step, pl.ds(1, 3)], r_send.at[step])
         copies = []
         for unit in range(8):
@@ -306,8 +301,9 @@
         for half in range(2 * STEPS):
             copies.append(core_copy(half // 2, half % 2, 0))
             for hop in range(1, 5):
-                copies += z_copies(half, hop)
-            if half < 9:
+                if half + hop < 12:
+                    copies += z_copies(half, hop)
+            if half < 8:
                 copies.append(core_copy(half // 2, half % 2, 1))
         for copy in copies:
             copy.wait_send()
@@ -323,18 +319,44 @@
         wd_copy(unit).start()
 
     def z_arrived(half):
+        if 0 <= half:
+            recv(z_copies(half, 4))
+            core_copy(half // 2, half % 2, 1).start()
+
+    def pair_here(half):
         step, pair = half // 2, half % 2
-        recv(z_copies(half, 4))
-        core_copy(step, pair, 1).start()
-        if pair == KEYS:
-            heads_wait(step, QUERIES)
         core_copy(step, pair, 0).wait_recv()
         core_copy(step, pair, 1).wait_recv()
         if pair == KEYS:
-            weigh(step)
+            heads_wait(step, QUERIES)
+
+    everywhere = pl.ds(0, 2)
+
+    def work(half, index):
+        if half < 0:
+            return
+        step = half // 2
+        if half % 2 == KEYS:
+            weigh(step, index)
         else:
-            attend(step)
-            home_start(step)
+            attend(step, index, [sums_over(step, index, rz, everywhere) for rz in range(2)])
+
+    def turn(at, after_first=(), after_second=(), after_last=()):
+        z_own(at)
+        z_forward(at - 3, 3)
+        z_arrived(at - 4)
+        for call in after_first:
+            call()
+        z_forward(at - 2, 2)
+        if at >= 4:
+            pair_here(at - 4)
+        work(at - 4, 1)
+        for call in after_second:
+            call()
+        z_forward(at - 1, 1)
+        work(at - 4, 0)
+        for call in after_last:
+            call()
 
     def y_ring(make, ring):
         for rel_zh in range(2):
@@ -344,97 +366,97 @@
         for rel_zh in range(2):
             recv(ring_of(make, rel_zh, ring))
 
+    def do(call, *args):
+        return lambda: call(*args)
+
+    def wz_ring(ring):
+        recv(both(wz_copy, ring - 1))
+        start(both(wz_copy, ring))
+
+    def weights_first():
+        recv(both(wz_copy, 3))
+        load_w.wait()
+        start(ring_of(wx_copy, 0, 0))
+        y_ring(wy_copy, 0)
+        y_ring(xb_copy, 0)
+        start(ring_of(wx_copy, 1, 0))
+
+    def rest_to_core(*units):
+        for unit in units:
+            db_copy(unit).start()
+
+    def from_core(*units):
+        for unit in units:
+            recv_other_core(unit)
+            recv_other_rest(unit)
+
+    def heads_more(*wanted):
+        for step, pair in wanted:
+            heads_start(step, pair)
+
+    heads_start(0, KEYS)
     start(both(wz_copy, 0))
-    heads_of(0)
+    heads_start(0, VALUES)
     acc[...] = jnp.zeros_like(acc)
-    heads_of(1)
-    recv(both(wz_copy, 0))
-    start(both(wz_copy, 1))
-    z_round(0)
-    recv(both(wz_copy, 1))
-    start(both(wz_copy, 2))
-    z_round(1)
-    recv(both(wz_copy, 2))
-    start(both(wz_copy, 3))
-    z_round(2)
-    recv(both(wz_copy, 3))
-    load_w.wait()
-    start(ring_of(wx_copy, 0, 0))
-    y_ring(wy_copy, 0)
-    y_ring(xb_copy, 0)
-    start(ring_of(wx_copy, 1, 0))
-    heads_of(2)
-    z_round(3)
-    y_recv(wy_copy, 0)
-    x_forward(0)
-    heads_of(3)
-    y_ring(wy_copy, 1)
-    z_round(4)
-    y_recv(xb_copy, 0)
-    y_ring(xb_copy, 1)
-    x_forward(1)
-    x_done(0)
-    z_arrived(0)
-    z_round(5)
-    x_forward(2)
-    x_done(1)
-    heads_of(4)
-    y_recv(xb_copy, 1)
-    y_recv(wy_copy, 1)
-    db_copy(0).start()
-    db_copy(1).start()
-    z_arrived(1)
-    z_round(6)
-    y_ring(yb_copy, 0)
-    x_forward(3)
-    x_done(2)
-    z_arrived(2)
-    z_round(7)
-    x_forward(4)
-    x_done(3)
-    z_arrived(3)
-    z_round(8)
-    x_forward(5)
-    x_done(4)
-    y_recv(yb_copy, 0)
-    y_ring(yb_copy, 1)
-    for unit in range(2, 6):
-        db_copy(unit).start()
-    z_arrived(4)
-    z_round(9)
-    x_forward(6)
-    x_done(5)
-    z_arrived(5)
-    z_round(10)
-    x_forward(7)
-    x_done(6)
-    y_recv(yb_copy, 1)
-    db_copy(6).start()
-    db_copy(7).start()
-    for unit in range(6):
-        recv_other_core(unit)
-        recv_other_rest(unit)
-    for step in range(2):
-        home_wait(step)
-    project(0, 3, 0, 2)
-    z_arrived(6)
-    z_round(11)
-    x_done(7)
-    home_wait(2)
-    project(0, 3, 2, 1)
-    z_arrived(7)
-    z_round(12)
-    for unit in range(6, 8):
-        recv_other_core(unit)
-        recv_other_rest(unit)
-    project(3, 1, 0, 3)
-    z_arrived(8)
-    home_wait(3)
-    project(0, 4, 3, 1)
-    sends_done()
+    wz_ring(1)
+    turn(0)
+    heads_start(1, KEYS)
+    wz_ring(2)
+    turn(1)
+    heads_start(1, VALUES)
+    wz_ring(3)
+    turn(2)
+    heads_start(0, QUERIES)
+    weights_first()
+    heads_start(2, KEYS)
+    turn(3, [do(heads_start, 2, VALUES)], [], [do(y_recv, wy_copy, 0), do(x_forward, 0)])
+    turn(
+        4,
+        [do(y_ring, wy_copy, 1), do(heads_more, (3, KEYS), (3, VALUES), (1, QUERIES)), do(y_recv, xb_copy, 0)],
+        [do(y_ring, xb_copy, 1), do(x_forward, 1)],
+        [do(x_done, 0)],
+    )
+    turn(
+        5,
+        [do(heads_more, (4, KEYS), (4, VALUES), (2, QUERIES))],
+        [do(x_forward, 2), do(x_done, 1)],
+        [do(y_recv, xb_copy, 1), do(y_recv, wy_copy, 1), do(rest_to_core, 0, 1), do(y_ring, yb_copy, 0)],
+    )
+    turn(6, [do(heads_more, (3, QUERIES), (4, QUERIES))], [do(x_forward, 3), do(x_done, 2)], [do(x_forward, 4)])
+    turn(7, [do(x_done, 3)], [do(x_done, 4)], [do(x_forward, 5)])
+    turn(
+        8,
+        [do(y_recv, yb_copy, 0), do(y_ring, yb_copy, 1)],
+        [do(rest_to_core, 2, 3, 4, 5), do(x_done, 5)],
+        [do(x_forward, 6)],
+    )
+    turn(
+        9,
+        [do(x_done, 6)],
+        [do(from_core, 0, 1, 2, 3, 4, 5)],
+        [do(x_forward, 7), do(home_wait, 0), do(project, 0, 3, 0, 1)],
+    )
+    turn(
+        10,
+        [do(y_recv, yb_copy, 1), do(rest_to_core, 6, 7), do(x_done, 7)],
+        [do(home_wait, 1)],
+        [do(project, 0, 3, 1, 1)],
+    )
+    turn(11, [do(from_core, 6, 7)], [do(home_wait, 2)], [do(project, 0, 4, 2, 1), do(project, 3, 1, 0, 2)])
+    turn(12, [do(sends_done)], [], [do(home_wait, 3), do(project, 0, 4, 3, 1)])
+    last = STEPS - 1
+    core_copy(last, VALUES, 0).wait_recv()
+    for index in range(2):
+        sums_ref[index], carry_ref[index] = sums_over(last, index, 0, everywhere)
     z_arrived(9)
-
-    last = STEPS - 1
+    for index in range(2):
+        sums, moved = sums_over(last, index, 1, pl.ds(0, 1))
+        sums_ref[index] += sums
+        carry_ref[index] += moved
+    core_copy(last, VALUES, 1).wait_recv()
+    for index in (1, 0):
+        attend(last, index, [(sums_ref[index], carry_ref[index]), sums_over(last, index, 1, pl.ds(1, 1))])
+
     home_wait(last)
 
     def finish(block, carry):
@@ -443,8 +465,13 @@
         return carry
 
     lax.fori_loop(0, 4, finish, 0)
+    for half, hop in ((8, 4), (9, 3), (9, 4)):
+        for copy in z_copies(half, hop):
+            copy.wait_send()
+    core_copy(last, KEYS, 1).wait_send()
     core_copy(last, VALUES, 1).wait_send()
-    await_bytes(ob.at[last, pl.ds(1, 3)], r_send.at[last])
+    for step in (last - 1, last):
+        await_bytes(ob.at[step, pl.ds(1, 3)], r_send.at[step])
 
     def drain(block, carry):
         for copy in out_copies(block):
@@ -461,10 +488,11 @@
     anywhere = pl.BlockSpec(memory_space=pl.ANY)
     return pl.pallas_call(
         kernel,
-        out_shape=(result, result, jax.ShapeDtypeStruct((2 * STEPS, 3, 2, 4, TOK, HEAD), low)),
+        out_shape=(result, result),
         in_specs=[anywhere] * 7,
-        out_specs=(anywhere, anywhere, anywhere),
+        out_specs=(anywhere, anywhere),
         scratch_shapes=[
+            pltpu.VMEM((2 * STEPS, 3, 2, 4, TOK, HEAD), low),
             pltpu.VMEM((STEPS, 2, 2, 4, 4, TOK, HEAD), low),
             pltpu.VMEM((STEPS, 2, 4, TOK, HEAD), low),
             pltpu.VMEM((STEPS, 4, 2, TOK, HEAD), low),
@@ -476,6 +504,8 @@
             pltpu.VMEM((2, 2 * TOK, 16 * TOK), low),
             pltpu.VMEM((2, 2 * TOK, 1), jnp.float32),
             pltpu.VMEM((2, 2 * TOK, 1), jnp.float32),
+            pltpu.VMEM((2, 2 * TOK, 2 * HEAD), jnp.float32),
+            pltpu.VMEM((2, 2 * TOK, HEAD), jnp.float32),
             dma((STEPS, 3)), dma((STEPS, 3)),
             dma((2 * STEPS, 4, 2)), dma((2 * STEPS, 4, 2)),
             dma((2 * STEPS, 2)), dma((2 * STEPS, 2)),
@@ -492,7 +522,7 @@
         compiler_params=pltpu.CompilerParams(
             collective_id=0, has_side_effects=True, vmem_limit_bytes=64 * 1024 * 1024
         ),
-    )(*arrays[:6], arrays[6].T)[:2]
+    )(*arrays[:6], arrays[6].T)
 
 
 def solution(mesh):

time: 164 us -> 160 us (0.976)
  Pallas kernels: 159 us -> 156 us
    pallas_call x1, Pallas kernels: 159 us -> 156 us  [per_device(): pl.pallas_call(kernel, out_shape=(result, result), in_specs=[anywhere] *...]
where the time goes in v3:
time: 160 us
  Pallas kernels  156 us (98%)
  local copies, waits for them, and re-layouts  3.62 us (2%)
    pallas_call x1, Pallas kernels, per_device(): pl.pallas_call(kernel, out_shape=(result, result), in_specs=[anywhere] *...  156 us
    unnamed x4, local copies, waits for them, and re-layouts  3.62 us

profile of v3, /device:TPU:1, one launch (start us, length us, event | category | flops | bytes accessed | tf_op | source)
XLA Modules:
  0.0 159.9 jit_solution(16178069762952208691)
XLA Ops:
  0.6 155.7 %shard_map.86 = (bf16[1,128,5120]{2,1,0:T(8,128)(2,1)}, bf16[1,128,5120]{2,1,0:T(8,128)(2,1)}) custom-call(bf16[1,128,2560]{2,1,0:T(8,128)(2,1)} %q_in.1, bf16[1,128,2560]{2,1,0:T(8,128)(2,1)} %k_in.1, bf16[1,128,2560]{2,1,0:T(8,128)(2,1)} %v_in.1, bf16[1,128,2560]{2,1,0:T(8,128)(2,1)} %qt_in.1, bf16[1,128,2560]{2,1,0:T(8,128)(2,1)} %kt_in.1, ...), custom_call_target="tpu_custom_call" | custom-call | tf_op jit(solution)/shard_map/pallas_call | solution.py:489
  156.3 0.0 copy-start
  156.3 2.6 %copy.11 = bf16[1,128,5120]{2,1,0:T(8,128)(2,1)} copy(bf16[1,128,5120]{2,1,0:T(8,128)(2,1)} %get-tuple-element.4) | data formatting | bytes 2621440
  158.9 0.0 copy-done
  158.9 1.1 copy.12
Async XLA Ops:
  156.3 2.6 %copy-start = (bf16[1,128,5120]{2,1,0:T(8,128)(2,1)S(1)}, bf16[1,128,5120]{2,1,0:T(8,128)(2,1)}, u32[]{:S(2)}) copy-start(bf16[1,128,5120]{2,1,0:T(8,128)(2,1)} %get-tuple-element.5) | copy-start | bytes 3932164

commit v4 on v3

--- a/solution.py
+++ b/solution.py
@@ -17,12 +17,12 @@
 
 
 def kernel(
-    q_in, k_in, v_in, qt_in, kt_in, vt_in, w_in, out, out_t,
-    relay, kvb, qb, ob, ab, wt, acc, stage, low_ref, moved_ref, total_ref, spread_ref, sums_ref, carry_ref,
+    q_in, k_in, v_in, qt_in, kt_in, vt_in, w_in, out, out_t, relay,
+    kvb, qb, ob, ab, wt, acc, low_ref, moved_ref, total_ref, spread_ref, sums_ref, carry_ref,
     a_send, a_recv, z_send, z_recv, c_send, c_recv, r_send, r_recv,
     wz_send, wz_recv, wy_send, wy_recv, wx_send, wx_recv, wd_send, wd_recv,
     xb_send, xb_recv, yb_send, yb_recv, db_send, db_recv,
-    l_sem, o_sem,
+    l_sem,
 ):
     dp = lax.axis_index("dp")
     uly = lax.axis_index("uly")
@@ -273,13 +273,6 @@
             return carry
 
         lax.fori_loop(0, blocks * steps, one, 0)
-
-    def out_copies(block):
-        columns = pl.ds(pl.multiple_of(block * 1280, 1280), 1280)
-        return [
-            pltpu.make_async_copy(stage.at[block, pl.ds(item * TOK, TOK)], ref.at[0, :, columns], o_sem.at[block, item])
-            for item, ref in enumerate((out, out_t))
-        ]
 
     def sends_done():
         for step in range(STEPS):
@@ -442,8 +435,8 @@
         [do(home_wait, 1)],
         [do(project, 0, 3, 1, 1)],
     )
-    turn(11, [do(from_core, 6, 7)], [do(home_wait, 2)], [do(project, 0, 4, 2, 1), do(project, 3, 1, 0, 2)])
-    turn(12, [do(sends_done)], [], [do(home_wait, 3), do(project, 0, 4, 3, 1)])
+    turn(11, [], [do(home_wait, 2)], [do(project, 0, 3, 2, 1)])
+    turn(12)
     last = STEPS - 1
     core_copy(last, VALUES, 0).wait_recv()
     for index in range(2):
@@ -456,12 +449,19 @@
     core_copy(last, VALUES, 1).wait_recv()
     for index in (1, 0):
         attend(last, index, [(sums_ref[index], carry_ref[index]), sums_over(last, index, 1, pl.ds(1, 1))])
+    from_core(6, 7)
+    project(3, 1, 0, 3)
+    home_wait(last - 1)
+    project(0, 4, last - 1, 1)
+    sends_done()
 
     home_wait(last)
 
     def finish(block, carry):
-        stage[block] = (acc[block] + product(block, last)).astype(jnp.bfloat16)
-        start(out_copies(block))
+        columns = pl.ds(pl.multiple_of(block * 1280, 1280), 1280)
+        sums = (acc[block] + product(block, last)).astype(jnp.bfloat16)
+        out[0, :, columns] = sums[:TOK]
+        out_t[0, :, columns] = sums[TOK:]
         return carry
 
     lax.fori_loop(0, 4, finish, 0)
@@ -473,33 +473,24 @@
     for step in (last - 1, last):
         await_bytes(ob.at[step, pl.ds(1, 3)], r_send.at[step])
 
-    def drain(block, carry):
-        for copy in out_copies(block):
-            copy.wait()
-        return carry
-
-    lax.fori_loop(0, 4, drain, 0)
-
 
 def per_device(*arrays):
     dma = pltpu.SemaphoreType.DMA
     low = jnp.bfloat16
-    result = jax.ShapeDtypeStruct((1, TOK, 5120), low)
+    result = pltpu.VMEM((1, TOK, 5120), low)
     anywhere = pl.BlockSpec(memory_space=pl.ANY)
     return pl.pallas_call(
         kernel,
-        out_shape=(result, result),
+        out_shape=(result, result, jax.ShapeDtypeStruct((2 * STEPS, 3, 2, 4, TOK, HEAD), low)),
         in_specs=[anywhere] * 7,
-        out_specs=(anywhere, anywhere),
+        out_specs=(pl.BlockSpec(memory_space=pltpu.VMEM),) * 2 + (anywhere,),
         scratch_shapes=[
-            pltpu.VMEM((2 * STEPS, 3, 2, 4, TOK, HEAD), low),
             pltpu.VMEM((STEPS, 2, 2, 4, 4, TOK, HEAD), low),
             pltpu.VMEM((STEPS, 2, 4, TOK, HEAD), low),
             pltpu.VMEM((STEPS, 4, 2, TOK, HEAD), low),
             pltpu.VMEM((STEPS, 4, 2, TOK, HEAD), low),
             pltpu.VMEM((4, 4, 4, 4, 80, 640), low),
             pltpu.VMEM((4, 2 * TOK, 1280), jnp.float32),
-            pltpu.VMEM((4, 2 * TOK, 1280), low),
             pltpu.VMEM((2, 2 * TOK, 16 * TOK), low),
             pltpu.VMEM((2, 2 * TOK, 16 * TOK), low),
             pltpu.VMEM((2, 2 * TOK, 1), jnp.float32),
@@ -517,12 +508,12 @@
             dma((2, 2, 2)), dma((2, 2, 2)),
             dma((2, 2, 2)), dma((2, 2, 2)),
             dma((8,)), dma((8,)),
-            dma, dma((4, 2)),
+            dma,
         ],
         compiler_params=pltpu.CompilerParams(
-            collective_id=0, has_side_effects=True, vmem_limit_bytes=64 * 1024 * 1024
+            collective_id=0, has_side_effects=True, vmem_limit_bytes=60 * 1024 * 1024
         ),
-    )(*arrays[:6], arrays[6].T)
+    )(*arrays[:6], arrays[6].T)[:2]
 
 
 def solution(mesh):

time: 160 us -> 158 us (0.988)
    unnamed x4 -> x2, local copies, waits for them, and re-layouts: 3.62 us -> 2.11 us
where the time goes in v4:
time: 158 us
  Pallas kernels  156 us (99%)
  local copies, waits for them, and re-layouts  2.11 us (1%)
    pallas_call x1, Pallas kernels, per_device(): pl.pallas_call(kernel, out_shape=(result, result, jax.ShapeDtypeStruct((2...  156 us

profile of v4, /device:TPU:1, one launch (start us, length us, event | category | flops | bytes accessed | tf_op | source)
XLA Modules:
  0.0 158.4 jit_solution(5344219934854386263)
XLA Ops:
  0.6 155.7 %shard_map.86 = (bf16[1,128,5120]{2,1,0:T(8,128)(2,1)S(1)}, bf16[1,128,5120]{2,1,0:T(8,128)(2,1)S(1)}, bf16[10,3,2,4,128,128]{5,4,3,2,1,0:T(8,128)(2,1)}) custom-call(bf16[1,128,2560]{2,1,0:T(8,128)(2,1)} %q_in.1, bf16[1,128,2560]{2,1,0:T(8,128)(2,1)} %k_in.1, bf16[1,128,2560]{2,1,0:T(8,128)(2,1)} %v_in.1, bf16[1,128,2560]{2,1,0:T(8,128)(2,1)} %qt_in.1, ...), custom_call_target="tpu_custom_call" | custom-call | tf_op jit(solution)/shard_map/pallas_call | solution.py:482
  156.3 1.1 copy.11
  157.4 1.1 copy.12

commit v5 on v4

--- a/solution.py
+++ b/solution.py
@@ -17,8 +17,8 @@
 
 
 def kernel(
-    q_in, k_in, v_in, qt_in, kt_in, vt_in, w_in, out, out_t, relay,
-    kvb, qb, ob, ab, wt, acc, low_ref, moved_ref, total_ref, spread_ref, sums_ref, carry_ref,
+    q_in, k_in, v_in, qt_in, kt_in, vt_in, w_in, out, out_t,
+    relay, kvb, qb, ob, ab, wt, acc, low_ref, moved_ref, total_ref, spread_ref, sums_ref, carry_ref,
     a_send, a_recv, z_send, z_recv, c_send, c_recv, r_send, r_recv,
     wz_send, wz_recv, wy_send, wy_recv, wx_send, wx_recv, wd_send, wd_recv,
     xb_send, xb_recv, yb_send, yb_recv, db_send, db_recv,
@@ -481,10 +481,11 @@
     anywhere = pl.BlockSpec(memory_space=pl.ANY)
     return pl.pallas_call(
         kernel,
-        out_shape=(result, result, jax.ShapeDtypeStruct((2 * STEPS, 3, 2, 4, TOK, HEAD), low)),
+        out_shape=(result, result),
         in_specs=[anywhere] * 7,
-        out_specs=(pl.BlockSpec(memory_space=pltpu.VMEM),) * 2 + (anywhere,),
+        out_specs=(pl.BlockSpec(memory_space=pltpu.VMEM),) * 2,
         scratch_shapes=[
+            pltpu.VMEM((2 * STEPS, 3, 2, 4, TOK, HEAD), low),
             pltpu.VMEM((STEPS, 2, 2, 4, 4, TOK, HEAD), low),
             pltpu.VMEM((STEPS, 2, 4, TOK, HEAD), low),
             pltpu.VMEM((STEPS, 4, 2, TOK, HEAD), low),
@@ -511,9 +512,9 @@
             dma,
         ],
         compiler_params=pltpu.CompilerParams(
-            collective_id=0, has_side_effects=True, vmem_limit_bytes=60 * 1024 * 1024
+            collective_id=0, has_side_effects=True, vmem_limit_bytes=61 * 1024 * 1024
         ),
-    )(*arrays[:6], arrays[6].T)[:2]
+    )(*arrays[:6], arrays[6].T)
 
 
 def solution(mesh):

time: 158 us -> 158 us (level)
  no operation moved by 1% of the time
where the time goes in v5:
time: 158 us; the launch traced here: 157 us
  Pallas kernels  155 us (98%)
  local copies, waits for them, and re-layouts  2.11 us (1%)
    pallas_call x1, Pallas kernels, per_device(): pl.pallas_call(kernel, out_shape=(result, result), in_specs=[anywhere] *...  155 us

profile of v5, /device:TPU:1, one launch (start us, length us, event | category | flops | bytes accessed | tf_op | source)
XLA Modules:
  0.0 157.5 jit_solution(1466588837679250950)
XLA Ops:
  0.6 154.7 %shard_map.86 = (bf16[1,128,5120]{2,1,0:T(8,128)(2,1)S(1)}, bf16[1,128,5120]{2,1,0:T(8,128)(2,1)S(1)}) custom-call(bf16[1,128,2560]{2,1,0:T(8,128)(2,1)} %q_in.1, bf16[1,128,2560]{2,1,0:T(8,128)(2,1)} %k_in.1, bf16[1,128,2560]{2,1,0:T(8,128)(2,1)} %v_in.1, bf16[1,128,2560]{2,1,0:T(8,128)(2,1)} %qt_in.1, bf16[1,128,2560]{2,1,0:T(8,128)(2,1)} %kt_in.1, ...), custom_call_target="tpu_custom_call" | custom-call | tf_op jit(solution)/shard_map/pallas_call | solution.py:482
  155.4 1.1 copy.11
  156.4 1.1 copy.12
